TPU v7x, 32 devices: a whole 2x2x4 slice. The times are simulated.
32 devices in a mesh: groups: 2 (over y), gx: 8 (over z, x), gy: 2 (over core).
Axes of the slice: x: 2, y: 2, z: 4, core: 2. Of those that a mesh axis runs over, the one named last changes fastest.
Arguments:
- activations: bfloat16 [128, 16384], P(('groups', 'gy'), 'gx'), parts along dimension 0, may hold values from -6 to 6
- qkv_weight: bfloat16 [16384, 18432], P('gx', 'gy'), may hold values from -0.046875 to 0.046875
- out_weight: bfloat16 [16384, 16384], P('gy', 'gx'), may hold values from -0.046875 to 0.046875
- key_cache: bfloat16 [128, 256, 8, 128], P(('groups', 'gx'), None, 'gy'), parts along dimension 0, may hold values from -600 to 600
- value_cache: bfloat16 [128, 256, 8, 128], P(('groups', 'gx'), None, 'gy'), parts along dimension 0, may hold values from -6 to 6
- lengths: int32 [128], P(('groups', 'gx')), parts along dimension 0, may hold values from 1 to 256, as said below
Outputs:
- attn_out: bfloat16 [128, 16384], P(('groups', 'gy'), 'gx'), parts along dimension 0
There are 2 independent parts, one for each index of `groups`. A program takes and returns all parts, laid end to end along the dimension named above; an argument that names none is the same for every part. Nothing has to cross between parts.
Inputs may be any that keep to these rules, and one draw needn't show every extreme that they name: `lengths`: each request's cached tokens; in every block of 8 requests held by one index of gx some request has all 256 slots filled.
All inputs are finite; a program needn't handle non-finite values.
Results may differ from a plain program's by a relative error of at most 0.015.
Values may be sent and summed in bfloat16 or wider, within the bound.
A program may use at most 128 MiB of HBM per device.

v0:
```python
import jax
import jax.numpy as jnp
from jax import lax
from jax.sharding import PartitionSpec as P


def rotate(vectors, positions):
    half_dim = vectors.shape[-1] // 2
    frequency = 500000.0 ** (-(jnp.arange(half_dim).astype(jnp.float32) * 2.0 / vectors.shape[-1]))
    angles = positions.astype(jnp.float32)[..., None] * frequency
    cosine = jnp.cos(angles)
    sine_part = jnp.sin(angles)
    lower_half = vectors[..., :half_dim]
    upper_half = vectors[..., half_dim:]
    return jnp.concatenate(
        [
            lower_half * cosine - upper_half * sine_part,
            upper_half * cosine + lower_half * sine_part,
        ],
        axis=-1,
    )


def attend(queries, new_key, new_value, keys, values, lengths):
    queries = rotate(queries.astype(jnp.float32), lengths[:, None, None]).astype(jnp.bfloat16)
    new_key = rotate(new_key.astype(jnp.float32), lengths[:, None]).astype(jnp.bfloat16)
    scaling = queries.shape[-1] ** (-0.5)
    scores = (
        jnp.einsum("rgqd,rpgd->rgqp", queries, keys, preferred_element_type=jnp.float32) * scaling
    )
    own_score = (
        jnp.einsum("rgqd,rgd->rgq", queries, new_key, preferred_element_type=jnp.float32) * scaling
    )
    visible = (jnp.arange(keys.shape[1])[None, :] < lengths[:, None])[:, None, None, :]
    masked = jnp.where(visible, scores, -1e30)
    highest = jnp.maximum(jnp.max(masked, axis=-1), own_score)
    raised = jnp.where(visible, jnp.exp(masked - highest[..., None]), 0.0)
    own_raised = jnp.exp(own_score - highest)
    denominator = jnp.sum(raised, axis=-1) + own_raised
    weights = (raised / denominator[..., None]).astype(jnp.bfloat16)
    own_weight = (own_raised / denominator).astype(jnp.bfloat16)
    blended = jnp.einsum("rgqp,rpgd->rgqd", weights, values, preferred_element_type=jnp.float32)
    blended = (
        blended
        + own_weight.astype(jnp.float32)[..., None] * new_value.astype(jnp.float32)[:, :, None, :]
    )
    return blended.astype(jnp.bfloat16)


def local(activations, qkv_weight, out_weight, key_cache, value_cache, lengths):
    rows_dev = key_cache.shape[0]
    head_groups = key_cache.shape[2]
    head_dim = key_cache.shape[3]
    all_rows = lax.all_gather(activations, "gy", axis=0, tiled=True)
    summed = lax.psum_scatter(
        jnp.dot(all_rows, qkv_weight, preferred_element_type=jnp.float32),
        "gx",
        scatter_dimension=0,
        tiled=True,
    )
    projected = summed.astype(jnp.bfloat16).reshape(rows_dev, head_groups, -1, head_dim)
    attended = attend(
        projected[:, :, :-2],
        projected[:, :, -2],
        projected[:, :, -1],
        key_cache,
        value_cache,
        lengths,
    )
    attended = attended.reshape(rows_dev, -1)
    partial_out = jnp.dot(
        lax.all_gather(attended, "gx", axis=0, tiled=True),
        out_weight,
        preferred_element_type=jnp.float32,
    )
    return lax.psum_scatter(partial_out.astype(jnp.bfloat16), "gy", scatter_dimension=0, tiled=True)


def solution(mesh):
    placed = (
        P(("groups", "gy"), "gx"),
        P("gx", "gy"),
        P("gy", "gx"),
        P(("groups", "gx"), None, "gy", None),
        P(("groups", "gx"), None, "gy", None),
        P(("groups", "gx")),
    )
    return jax.shard_map(
        local, mesh=mesh, in_specs=placed, out_specs=P(("groups", "gy"), "gx"), check_vma=False
    )
```

profile of v0, /device:TPU:0, one launch (start us, length us, event | category | flops | bytes accessed | tf_op | source)
XLA Modules:
  0.0 171.5 jit_solution(14467658440540007544)
XLA Ops:
  6.5 0.0 copy-start
  6.5 0.0 reduce-scatter.3.cloned.1.call-start
  6.5 2.4 %all_gather.6 = bf16[64,2048]{1,0:T(8,128)(2,1)S(1)} all-gather(bf16[32,2048]{1,0:T(8,128)(2,1)} %param.6), channel_id=1, replica_groups=mesh['groups'=2,'gx'=8,'gy'=2] {'gy'}, dimensions={0}, use_global_device_ids=true | all-gather | bytes 393216 | tf_op jit(solution)/shard_map/all_gather | solution.py:54
  9.0 16.5 %fusion.31 = f32[64,9216]{1,0:T(8,128)} fusion(bf16[64,2048]{1,0:T(8,128)(2,1)S(1)} %all_gather.6, bf16[2048,9216]{1,0:T(8,128)(2,1)} %param.7), kind=kOutput, calls=%fused_computation.43 | convolution fusion | flops 2415919104 | bytes 40370176 | tf_op jit(solution)/shard_map/dot_general | solution.py:56
  25.5 0.0 copy-start.2
  25.5 0.0 reduce-scatter.3.cloned.1.call-update
  25.5 0.0 all-gather.2.cloned.1.call-start
  25.6 0.6 copy-done.2
  26.2 0.1 iota_compare_fusion
  26.2 0.1 multiply_cosine_fusion
  26.3 71.0 %reduce-scatter.3.cloned.1.call-done = f32[8,9216]{1,0:T(8,128)} async-done(((f32[64,9216]{1,0:T(8,128)}), f32[8,9216]{1,0:T(8,128)}) %reduce-scatter.3.cloned.1.call-update) | async-done | bytes 294928 | tf_op jit(solution)/shard_map/reduce_scatter | solution.py:55
  97.3 1.0 convert_element_type.49
  98.3 0.1 subtract_convert_fusion.1
  98.4 0.0 copy-start.3
  98.4 0.2 subtract_convert_fusion
  98.6 0.1 maximum_bitcast_fusion
  98.6 0.2 fusion.21
  98.9 0.0 copy-done
  98.9 0.8 fusion.30
  99.7 0.3 fusion.16
  100.1 0.0 copy-done.3
  100.1 0.5 fusion.13
  100.6 0.8 copy.33
  101.3 0.0 all-gather.2.cloned.1.call-update
  101.3 0.0 reduce-scatter.5.cloned.1.call-start
  101.4 39.3 %all-gather.2.cloned.1.call-done = bf16[64,8192]{1,0:T(8,128)(2,1)} async-done(((bf16[8,8192]{1,0:T(8,128)(2,1)}), bf16[64,8192]{1,0:T(8,128)(2,1)}) %all-gather.2.cloned.1.call-update) | async-done | bytes 1048592 | tf_op jit(solution)/shard_map/all_gather | solution.py:72
  140.7 0.0 copy-start.1
  140.7 17.6 %convolution_convert_fusion = bf16[64,2048]{1,0:T(8,128)(2,1)} fusion(bf16[64,8192]{1,0:T(8,128)(2,1)} %all-gather.2.cloned.1.call-done, bf16[8192,2048]{1,0:T(8,128)(2,1)} %param.8), kind=kOutput, calls=%fused_computation | convolution fusion | flops 2147614720 | bytes 34865152 | tf_op jit(solution)/shard_map/dot_general | solution.py:71
  158.3 0.0 reduce-scatter.5.cloned.1.call-update
  158.4 6.6 %reduce-scatter.5.cloned.1.call-done = bf16[32,2048]{1,0:T(8,128)(2,1)} async-done(((bf16[64,2048]{1,0:T(8,128)(2,1)}), bf16[32,2048]{1,0:T(8,128)(2,1)}) %reduce-scatter.5.cloned.1.call-update) | async-done | bytes 131088 | tf_op jit(solution)/shard_map/reduce_scatter | solution.py:76
  164.9 0.0 copy-done.1
  (8 shorter events, 0.1 us)
Async XLA Ops:
  6.5 92.4 %copy-start = (bf16[8,256,4,128]{3,2,1,0:T(4,128)(2,1)S(1)}, bf16[8,256,4,128]{3,2,1,0:T(4,128)(2,1)}, u32[]{:S(2)}) copy-start(bf16[8,256,4,128]{3,2,1,0:T(4,128)(2,1)} %param.9) | copy-start | bytes 6291460
  6.5 90.8 %reduce-scatter.3.cloned.1.call-start = ((), (), s32[]{:S(2)}) async-start(), calls=%async_computation.2 | async-start | bytes 2654208 | tf_op jit(solution)/shard_map/reduce_scatter | solution.py:55
  25.5 0.7 copy-start.2
  25.5 115.2 %all-gather.2.cloned.1.call-start = ((), (), s32[]{:S(2)}) async-start(), calls=%async_computation.3 | async-start | bytes 1179648 | tf_op jit(solution)/shard_map/all_gather | solution.py:72
  98.4 1.7 copy-start.3
  101.3 63.6 %reduce-scatter.5.cloned.1.call-start = ((), (), s32[]{:S(2)}) async-start(), calls=%async_computation.4 | async-start | bytes 393216 | tf_op jit(solution)/shard_map/reduce_scatter | solution.py:76
  140.7 24.2 %copy-start.1 = (bf16[8,256,4,128]{3,2,1,0:T(4,128)(2,1)S(1)}, bf16[8,256,4,128]{3,2,1,0:T(4,128)(2,1)}, u32[]{:S(2)}) copy-start(bf16[8,256,4,128]{3,2,1,0:T(4,128)(2,1)} %param.9) | copy-start | bytes 6291460
Sparse Core Ops, SparseCore 0:
  25.6 71.6 reduce-scatter.2
  101.5 39.1 all-gather.1
  158.5 6.4 reduce-scatter.4
where the time goes:
time: 172 us; the launch traced here: 171 us
  waiting for transfers between devices  117 us (68%)
  matrix products  35.7 us (21%)
  between operations  13.2 us (8%)
  blocking collectives  2.42 us (1%)
  other arithmetic  1.82 us (1%)
    reduce_scatter x1, waiting for transfers between devices, local(): lax.psum_scatter(jnp.dot(all_rows, qkv_weight, preferred_element_type=jnp...  71 us
    all_gather x1, waiting for transfers between devices, local(): lax.all_gather(attended, 'gx', axis=0, tiled=True)  39.3 us
    dot_general x1, matrix products, local(): jnp.dot(lax.all_gather(attended, 'gx', axis=0, tiled=True), out_weight, p...  17.6 us
    dot_general x1, matrix products, local(): jnp.dot(all_rows, qkv_weight, preferred_element_type=jnp.float32)  16.5 us
    reduce_scatter x1, waiting for transfers between devices, local(): lax.psum_scatter(partial_out.astype(jnp.bfloat16), 'gy', scatter_dimensio...  6.58 us
  transfers between devices with their start and end apart: 3, of which 3 were waited for; matrix products, arithmetic and copies ran while one was open for 0% of the time, Pallas kernels for 0%

commit v1 on v0

--- a/solution.py
+++ b/solution.py
@@ -1,7 +1,314 @@
+import functools
+
 import jax
 import jax.numpy as jnp
 from jax import lax
+from jax.experimental import pallas as pl
+from jax.experimental.pallas import tpu as pltpu
 from jax.sharding import PartitionSpec as P
+
+MESH = pl.DeviceIdType.MESH
+XN, ZN = 2, 4
+TILE = 256
+SLOTS = 4
+
+
+def fused_kernel(
+    dims, act_hbm, wq_hbm, wo_hbm, key_hbm, val_hbm, cos_ref, sin_ref, len_ref, out_ref,
+    act, wbuf, wo, keys, vals, xsend, xkeep, xrecv, zbuf, zrecv, proj, qrows, score, orows,
+    att, lhs, acc, psend, precv,
+    act_sem, w_sem, wo_sem, kv_sem, xs_sem, xr_sem, zs_sem, zr_sem,
+    azs_sem, azr_sem, axs_sem, axr_sem, ps_sem, pr_sem,
+):
+    groups, gq, hd, piece, pieces, rows_dev = dims
+    rows = act.shape[0]
+    half_rows = rows // 2
+    gx = lax.axis_index("gx")
+    gy = lax.axis_index("gy")
+    x = lax.rem(gx, XN)
+    z = lax.div(gx, XN)
+    xpeer = z * XN + (1 - x)
+    ypeer = 1 - gy
+
+    def zpeer(d):
+        return lax.rem(z + d, ZN) * XN + x
+
+    def zfrom(d):
+        return lax.rem(z + ZN - d, ZN) * XN + x
+
+    def w_copy(i):
+        cols = pl.ds(pl.multiple_of(i * piece, piece), piece)
+        slot = lax.rem(i, SLOTS)
+        return pltpu.make_async_copy(wq_hbm.at[:, cols], wbuf.at[slot], w_sem.at[slot])
+
+    group_width = gq * hd
+
+    def wo_copy(j):
+        part = pl.ds(pl.multiple_of(j * group_width, group_width), group_width)
+        return pltpu.make_async_copy(wo_hbm.at[part], wo.at[part], wo_sem.at[j])
+
+    key_copy = pltpu.make_async_copy(key_hbm, keys, kv_sem.at[0])
+    val_copy = pltpu.make_async_copy(val_hbm, vals, kv_sem.at[1])
+
+    def x_copy(i):
+        return pltpu.make_async_remote_copy(
+            xsend.at[i], xrecv.at[i], xs_sem.at[i], xr_sem.at[i],
+            device_id={"gx": xpeer}, device_id_type=MESH)
+
+    def z_copy(i, d):
+        return pltpu.make_async_remote_copy(
+            zbuf.at[i, lax.rem(z + d, ZN)], zrecv.at[i, d - 1], zs_sem.at[i, d - 1],
+            zr_sem.at[i, d - 1], device_id={"gx": zpeer(d)}, device_id_type=MESH)
+
+    def az_copy(j, d):
+        return pltpu.make_async_remote_copy(
+            att.at[j, gx], att.at[j, gx], azs_sem.at[j, d - 1], azr_sem.at[j, d - 1],
+            device_id={"gx": zpeer(d)}, device_id_type=MESH)
+
+    def az_arrival(j, d):
+        return pltpu.make_async_remote_copy(
+            att.at[j, zfrom(d)], att.at[j, zfrom(d)], azs_sem.at[j, d - 1], azr_sem.at[j, d - 1],
+            device_id={"gx": zpeer(d)}, device_id_type=MESH)
+
+    def ax_copy(j, d):
+        return pltpu.make_async_remote_copy(
+            att.at[j, zfrom(d)], att.at[j, zfrom(d)], axs_sem.at[j, d], axr_sem.at[j, d],
+            device_id={"gx": xpeer}, device_id_type=MESH)
+
+    def ax_arrival(j, d):
+        block = lax.rem(z + ZN - d, ZN) * XN + (1 - x)
+        return pltpu.make_async_remote_copy(
+            att.at[j, block], att.at[j, block], axs_sem.at[j, d], axr_sem.at[j, d],
+            device_id={"gx": xpeer}, device_id_type=MESH)
+
+    for i in range(SLOTS):
+        w_copy(i).start()
+    mine = pl.ds(pl.multiple_of(gy * half_rows, half_rows), half_rows)
+    theirs = pl.ds(pl.multiple_of(ypeer * half_rows, half_rows), half_rows)
+    own_act = pltpu.make_async_copy(act_hbm, act.at[mine], act_sem.at[0])
+    own_act.start()
+
+    barrier = pltpu.get_barrier_semaphore()
+    for d in range(1, ZN):
+        pl.semaphore_signal(barrier, inc=1, device_id={"gx": zpeer(d)}, device_id_type=MESH)
+    pl.semaphore_signal(barrier, inc=1, device_id={"gx": xpeer}, device_id_type=MESH)
+    pl.semaphore_signal(barrier, inc=1, device_id={"gy": ypeer}, device_id_type=MESH)
+    pl.semaphore_wait(barrier, ZN + 1)
+
+    peer_act = pltpu.make_async_remote_copy(
+        act_hbm, act.at[mine], act_sem.at[1], act_sem.at[2],
+        device_id={"gy": ypeer}, device_id_type=MESH)
+    peer_act.start()
+    key_copy.start()
+    val_copy.start()
+    acc[...] = jnp.zeros_like(acc)
+    own_act.wait()
+    peer_act.wait()
+
+    def project(j):
+        def one(p, _):
+            i = j * pieces + p
+            slot = lax.rem(i, SLOTS)
+            w_copy(i).wait()
+            for t in range(piece // TILE):
+                cols = pl.ds(t * TILE, TILE)
+                part = jnp.dot(act[...], wbuf[slot, :, cols], preferred_element_type=jnp.float32)
+                part = part.reshape(ZN, XN, rows_dev, TILE)
+                first, second = part[:, 0], part[:, 1]
+                xkeep[i, :, :, cols] = jnp.where(x == 0, first, second)
+                xsend[i, :, :, cols] = jnp.where(x == 0, second, first)
+            x_copy(i).start()
+
+            @pl.when(i + SLOTS < groups * pieces)
+            def _():
+                w_copy(i + SLOTS).start()
+            return 0
+        lax.fori_loop(0, pieces, one, 0)
+        wo_copy(j).start()
+
+    def across_x(j):
+        def one(p, _):
+            i = j * pieces + p
+            x_copy(i).wait_recv()
+            zbuf[i] = xkeep[i] + xrecv[i]
+            for d in range(1, ZN):
+                z_copy(i, d).start()
+            return 0
+        lax.fori_loop(0, pieces, one, 0)
+
+    def attention(j):
+        for p in range(pieces):
+            i = j * pieces + p
+            for d in range(1, ZN):
+                z_copy(i, d).wait_recv()
+            total = zbuf[i, z] + zrecv[i, 0] + zrecv[i, 1] + zrecv[i, 2]
+            proj[:, p * piece:(p + 1) * piece] = total.astype(jnp.bfloat16).astype(jnp.float32)
+
+        def turned(h):
+            v = proj[:, h * hd:(h + 1) * hd]
+            swapped = jnp.concatenate([v[:, hd // 2:], v[:, :hd // 2]], axis=1)
+            r = v * cos_ref[...] + swapped * sin_ref[...]
+            return r.astype(jnp.bfloat16).astype(jnp.float32)
+
+        for h in range(gq):
+            qrows[h * rows_dev:(h + 1) * rows_dev, :] = turned(h)
+        new_key = turned(gq)
+        new_value = proj[:, (gq + 1) * hd:(gq + 2) * hd]
+        scaling = hd ** -0.5
+        own = []
+        for r in range(rows_dev):
+            q = qrows[pl.ds(r, gq, stride=rows_dev), :]
+            score[r * gq:(r + 1) * gq, :] = lax.dot_general(
+                q.astype(jnp.bfloat16), keys[r], (((1,), (1,)), ((), ())),
+                preferred_element_type=jnp.float32) * scaling
+            own.append(jnp.sum(q * new_key[r:r + 1, :], axis=1, keepdims=True) * scaling)
+        own = jnp.concatenate(own, axis=0)
+        column = lax.broadcasted_iota(jnp.int32, score.shape, 1)
+        seen = (column < len_ref[:, :1]) & (lax.rem(column, groups) == j)
+        masked = jnp.where(seen, score[...], -1e30)
+        highest = jnp.maximum(jnp.max(masked, axis=1, keepdims=True), own)
+        raised = jnp.where(seen, jnp.exp(masked - highest), 0.0)
+        own_raised = jnp.exp(own - highest)
+        denominator = jnp.sum(raised, axis=1, keepdims=True) + own_raised
+        weights = (raised / denominator).astype(jnp.bfloat16)
+        own_weight = (own_raised / denominator).astype(jnp.bfloat16).astype(jnp.float32)
+        for r in range(rows_dev):
+            part = slice(r * gq, (r + 1) * gq)
+            blended = jnp.dot(weights[part], vals[r], preferred_element_type=jnp.float32)
+            orows[pl.ds(r, gq, stride=rows_dev), :] = blended + own_weight[part] * new_value[r:r + 1, :]
+        att[j, gx] = orows[...].astype(jnp.bfloat16)
+        for d in range(1, ZN):
+            az_copy(j, d).start()
+        ax_copy(j, 0).start()
+
+    def relay(j):
+        for d in range(1, ZN):
+            az_arrival(j, d).wait_recv()
+            ax_copy(j, d).start()
+
+    def output(j):
+        for d in range(ZN):
+            ax_arrival(j, d).wait_recv()
+        for b in range(XN * ZN // 2):
+            pair = []
+            for s in range(2):
+                block = att[j, 2 * b + s].astype(jnp.float32)
+                pair.append(jnp.concatenate(
+                    [block[h * rows_dev:(h + 1) * rows_dev] for h in range(gq)], axis=1))
+            lhs[2 * b * rows_dev:2 * (b + 1) * rows_dev, :] = jnp.concatenate(
+                pair, axis=0).astype(jnp.bfloat16)
+        wo_copy(j).wait()
+        depth = pl.ds(pl.multiple_of(j * group_width, group_width), group_width)
+
+        def one(n, _):
+            cols = pl.ds(pl.multiple_of(n * TILE, TILE), TILE)
+            acc[:, cols] += jnp.dot(lhs[...], wo[depth, cols], preferred_element_type=jnp.float32)
+            return 0
+        lax.fori_loop(0, acc.shape[1] // TILE, one, 0)
+
+    def step(t, _):
+        for delay, stage in enumerate((project, across_x, attention, relay, output)):
+            if delay == 2:
+                @pl.when(t == 2)
+                def _():
+                    key_copy.wait()
+                    val_copy.wait()
+
+            @pl.when((t >= delay) & (t < groups + delay))
+            def _(stage=stage, delay=delay):
+                stage(t - delay)
+        return 0
+    lax.fori_loop(0, groups + 4, step, 0)
+
+    psend[...] = acc[theirs, :].astype(jnp.bfloat16)
+    last = pltpu.make_async_remote_copy(
+        psend, precv, ps_sem, pr_sem, device_id={"gy": ypeer}, device_id_type=MESH)
+    last.start()
+    last.wait_recv()
+    out_ref[...] = (acc[mine, :] + precv[...].astype(jnp.float32)).astype(jnp.bfloat16)
+    last.wait_send()
+
+    def drain(j, _):
+        for p in range(pieces):
+            i = j * pieces + p
+            x_copy(i).wait_send()
+            for d in range(1, ZN):
+                z_copy(i, d).wait_send()
+        for d in range(1, ZN):
+            az_copy(j, d).wait_send()
+        for d in range(ZN):
+            ax_copy(j, d).wait_send()
+        return 0
+    lax.fori_loop(0, groups, drain, 0)
+
+
+def fused(activations, qkv_weight, out_weight, key_cache, value_cache, lengths):
+    rows_dev, context, groups, hd = key_cache.shape
+    half_rows, depth = activations.shape
+    rows = 2 * half_rows
+    qkv_cols = qkv_weight.shape[1]
+    heads_in = out_weight.shape[0]
+    width = out_weight.shape[1]
+    gq = heads_in // (groups * hd)
+    block = (gq + 2) * hd
+    pieces = 3
+    piece = block // pieces
+    n = groups * pieces
+    bf16, f32 = jnp.bfloat16, jnp.float32
+
+    half = hd // 2
+    frequency = 500000.0 ** (-(jnp.arange(half).astype(f32) * 2.0 / hd))
+    angles = lengths.astype(f32)[:, None] * frequency
+    cosine, sine = jnp.cos(angles), jnp.sin(angles)
+    cosine = jnp.concatenate([cosine, cosine], axis=1)
+    sine = jnp.concatenate([-sine, sine], axis=1)
+    limits = jnp.broadcast_to(jnp.repeat(lengths * groups, gq)[:, None], (rows_dev * gq, 128))
+
+    anywhere = pl.BlockSpec(memory_space=pl.ANY)
+    vmem = pl.BlockSpec(memory_space=pltpu.VMEM)
+    dma = pltpu.SemaphoreType.DMA
+    return pl.pallas_call(
+        functools.partial(fused_kernel, (groups, gq, hd, piece, pieces, rows_dev)),
+        out_shape=jax.ShapeDtypeStruct((half_rows, width), bf16),
+        in_specs=[anywhere] * 5 + [vmem] * 3,
+        out_specs=vmem,
+        scratch_shapes=[
+            pltpu.VMEM((rows, depth), bf16),
+            pltpu.VMEM((SLOTS, depth, piece), bf16),
+            pltpu.VMEM((heads_in, width), bf16),
+            pltpu.VMEM((rows_dev, context * groups, hd), bf16),
+            pltpu.VMEM((rows_dev, context * groups, hd), bf16),
+            pltpu.VMEM((n, ZN, rows_dev, piece), f32),
+            pltpu.VMEM((n, ZN, rows_dev, piece), f32),
+            pltpu.VMEM((n, ZN, rows_dev, piece), f32),
+            pltpu.VMEM((n, ZN, rows_dev, piece), f32),
+            pltpu.VMEM((n, ZN - 1, rows_dev, piece), f32),
+            pltpu.VMEM((rows_dev, block), f32),
+            pltpu.VMEM((gq * rows_dev, hd), f32),
+            pltpu.VMEM((gq * rows_dev, context * groups), f32),
+            pltpu.VMEM((gq * rows_dev, hd), f32),
+            pltpu.VMEM((groups, XN * ZN, gq * rows_dev, hd), bf16),
+            pltpu.VMEM((rows, gq * hd), bf16),
+            pltpu.VMEM((rows, width), f32),
+            pltpu.VMEM((half_rows, width), bf16),
+            pltpu.VMEM((half_rows, width), bf16),
+            dma((3,)), dma((SLOTS,)), dma((groups,)), dma((2,)),
+            dma((n,)), dma((n,)), dma((n, ZN - 1)), dma((n, ZN - 1)),
+            dma((groups, ZN - 1)), dma((groups, ZN - 1)), dma((groups, ZN)), dma((groups, ZN)),
+            dma, dma,
+        ],
+        compiler_params=pltpu.CompilerParams(
+            collective_id=0, has_side_effects=True, vmem_limit_bytes=63 * 1024 * 1024),
+        cost_estimate=pl.CostEstimate(
+            flops=2 * rows * (depth * qkv_cols + heads_in * width),
+            bytes_accessed=2 * (depth * qkv_cols + heads_in * width), transcendentals=0),
+        name="fused_attention",
+    )(
+        activations, qkv_weight, out_weight,
+        key_cache.reshape(rows_dev, context * groups, hd),
+        value_cache.reshape(rows_dev, context * groups, hd),
+        cosine, sine, limits,
+    )
 
 
 def rotate(vectors, positions):
@@ -85,6 +392,7 @@
         P(("groups", "gx"), None, "gy", None),
         P(("groups", "gx")),
     )
+    chosen = fused if mesh.shape["gx"] == XN * ZN and mesh.shape["gy"] == 2 else local
     return jax.shard_map(
-        local, mesh=mesh, in_specs=placed, out_specs=P(("groups", "gy"), "gx"), check_vma=False
-    )
+        chosen, mesh=mesh, in_specs=placed, out_specs=P(("groups", "gy"), "gx"), check_vma=False
+    )

time: 172 us -> 66.2 us (0.38)
  waiting for transfers between devices: 117 us -> 0 us
  Pallas kernels: 0 us -> 62.1 us
  matrix products: 35.7 us -> 0 us
  between operations: 13.2 us -> 0.01 us
  blocking collectives: 2.42 us -> 0 us
    reduce_scatter x2 -> x0, waiting for transfers between devices: 77.5 us -> none  [the longest x1 71 us: local(): lax.psum_scatter(jnp.dot(all_rows, qkv_weight, preferred_element_type=jnp...]
    pallas_call x0 -> x1, Pallas kernels: none -> 62.1 us  [fused(): pl.pallas_call(functools.partial(fused_kernel, (groups, gq, hd, piece, pi...]
    all_gather x1 -> x0, waiting for transfers between devices: 39.3 us -> none  [local(): lax.all_gather(attended, 'gx', axis=0, tiled=True)]
    dot_general x5 -> x0, matrix products: 35.7 us -> none  [the longest x1 17.6 us: local(): jnp.dot(lax.all_gather(attended, 'gx', axis=0, tiled=True), out_weight, p...]
    all_gather x1 -> x0, blocking collectives: 2.42 us -> none  [local(): all_rows = lax.all_gather(activations, 'gy', axis=0, tiled=True)]
  transfers between devices with their start and end apart: 3 -> 0, of which waited for: 3 -> 0; matrix products, arithmetic and copies ran while one was open for 0% -> 0% of each run, Pallas kernels for 0% -> 0%
where the time goes in v1:
time: 66.2 us; the launch traced here: 66 us
  Pallas kernels  62.1 us (94%)
  local copies, waits for them, and re-layouts  2.43 us (4%)
  other arithmetic  1.53 us (2%)
    pallas_call x1, Pallas kernels, fused(): pl.pallas_call(functools.partial(fused_kernel, (groups, gq, hd, piece, pi...  62.1 us
    unnamed x1, local copies, waits for them, and re-layouts  1.57 us

profile of v1, /device:TPU:0, one launch (start us, length us, event | category | flops | bytes accessed | tf_op | source)
XLA Modules:
  0.0 66.0 jit_solution(4848798740326678127)
XLA Ops:
  0.0 0.7 %broadcast_multiply_fusion = (s32[8]{0:T(128)S(1)}, f32[8]{0:T(128)S(1)}) fusion(s32[8]{0:T(128)} %param.11), kind=kLoop, calls=%fused_computation.6 | loop fusion | flops 16 | bytes 96 | tf_op jit(solution)/shard_map/mul | solution.py:265
  0.7 0.1 broadcast_in_dim.12
  0.8 0.1 broadcast_in_dim.13
  0.9 0.1 fusion
  1.0 0.7 %pad_maximum_fusion = (f32[8,128]{1,0:T(8,128)}, f32[8,128]{1,0:T(8,128)}) fusion(f32[8,64]{1,0:T(8,128)S(1)} %get-tuple-element.7, f32[8,64]{1,0:T(8,128)S(1)} %get-tuple-element.6, f32[8,64]{1,0:T(8,128)S(1)} %get-tuple-element.5), kind=kLoop, calls=%fused_computation.2 | loop fusion | flops 2048 | bytes 14336 | tf_op jit(solution)/shard_map/concatenate | solution.py:263
  1.7 0.7 %broadcast_in_dim.14.len_ref = s32[128,128]{1,0:T(8,128)} broadcast(s32[128]{0:T(128)S(1)} %broadcast_in_dim.13), dimensions={0} | broadcast | bytes 66048 | tf_op jit(solution)/shard_map/broadcast_in_dim | solution.py:265
  2.4 62.1 %fused_attention.1 = bf16[32,2048]{1,0:T(8,128)(2,1)} custom-call(bf16[32,2048]{1,0:T(8,128)(2,1)} %act_hbm.1, bf16[2048,9216]{1,0:T(8,128)(2,1)} %wq_hbm.1, bf16[8192,2048]{1,0:T(8,128)(2,1)} %wo_hbm.1, bf16[8,1024,128]{2,1,0:T(8,128)(2,1)} %bitcast.2, bf16[8,1024,128]{2,1,0:T(8,128)(2,1)} %bitcast.3, f32[8,128]{1,0:T(8,128)} %get-tuple-element.10.cos_ref, ...), custom_call_target="tpu_custom_call" | custom-call | flops 4563402752 | bytes 71303168 | tf_op jit(solution)/shard_map/fused_attention/pallas_call | solution.py:270
  64.5 1.6 %copy.8 = bf16[32,2048]{1,0:T(8,128)(2,1)} copy(bf16[32,2048]{1,0:T(8,128)(2,1)} %fused_attention.1) | data formatting | bytes 262144
  (1 shorter events, 0.0 us)

commit v2 on v1

--- a/solution.py
+++ b/solution.py
@@ -1,4 +1,5 @@
 import functools
+import math
 
 import jax
 import jax.numpy as jnp
@@ -14,8 +15,8 @@
 
 
 def fused_kernel(
-    dims, act_hbm, wq_hbm, wo_hbm, key_hbm, val_hbm, cos_ref, sin_ref, len_ref, out_ref,
-    act, wbuf, wo, keys, vals, xsend, xkeep, xrecv, zbuf, zrecv, proj, qrows, score, orows,
+    dims, act_hbm, wq_hbm, wo_hbm, key_hbm, val_hbm, len_ref, out_ref,
+    act, wbuf, wo, keys, vals, xsend, xkeep, xrecv, zbuf, zrecv, proj, qrows, score, orows, split, cos_ref, sin_ref,
     att, lhs, acc, psend, precv,
     act_sem, w_sem, wo_sem, kv_sem, xs_sem, xr_sem, zs_sem, zr_sem,
     azs_sem, azr_sem, axs_sem, axr_sem, ps_sem, pr_sem,
@@ -102,6 +103,15 @@
     key_copy.start()
     val_copy.start()
     acc[...] = jnp.zeros_like(acc)
+    row = lax.broadcasted_iota(jnp.int32, cos_ref.shape, 0)
+    lane = lax.broadcasted_iota(jnp.int32, cos_ref.shape, 1)
+    position = jnp.zeros(cos_ref.shape, jnp.int32)
+    for r in range(rows_dev):
+        position = jnp.where(row == r, len_ref[r], position)
+    index = lax.rem(lane, hd // 2).astype(jnp.float32)
+    angle = position.astype(jnp.float32) * jnp.exp(index * (-2.0 * math.log(500000.0) / hd))
+    cos_ref[...] = jnp.cos(angle)
+    sin_ref[...] = jnp.where(lane < hd // 2, -1.0, 1.0) * jnp.sin(angle)
     own_act.wait()
     peer_act.wait()
 
@@ -136,6 +146,20 @@
             return 0
         lax.fori_loop(0, pieces, one, 0)
 
+    def separate():
+        key_copy.wait()
+        val_copy.wait()
+
+        def one(r, _):
+            for cache in (keys, vals):
+                split[...] = cache[r].astype(jnp.float32)
+                context = split.shape[0] // groups
+                for g in range(groups):
+                    cache[r, g * context:(g + 1) * context, :] = split[
+                        pl.ds(g, context, stride=groups), :].astype(jnp.bfloat16)
+            return 0
+        lax.fori_loop(0, rows_dev, one, 0)
+
     def attention(j):
         for p in range(pieces):
             i = j * pieces + p
@@ -156,25 +180,27 @@
         new_value = proj[:, (gq + 1) * hd:(gq + 2) * hd]
         scaling = hd ** -0.5
         own = []
+        context = score.shape[1]
+        mine_keys = pl.ds(pl.multiple_of(j * context, context), context)
+        column = lax.broadcasted_iota(jnp.int32, (gq, context), 1)
         for r in range(rows_dev):
             q = qrows[pl.ds(r, gq, stride=rows_dev), :]
-            score[r * gq:(r + 1) * gq, :] = lax.dot_general(
-                q.astype(jnp.bfloat16), keys[r], (((1,), (1,)), ((), ())),
+            seen = lax.dot_general(
+                q.astype(jnp.bfloat16), keys[r, mine_keys], (((1,), (1,)), ((), ())),
                 preferred_element_type=jnp.float32) * scaling
+            score[r * gq:(r + 1) * gq, :] = jnp.where(column < len_ref[r], seen, -1e30)
             own.append(jnp.sum(q * new_key[r:r + 1, :], axis=1, keepdims=True) * scaling)
         own = jnp.concatenate(own, axis=0)
-        column = lax.broadcasted_iota(jnp.int32, score.shape, 1)
-        seen = (column < len_ref[:, :1]) & (lax.rem(column, groups) == j)
-        masked = jnp.where(seen, score[...], -1e30)
+        masked = score[...]
         highest = jnp.maximum(jnp.max(masked, axis=1, keepdims=True), own)
-        raised = jnp.where(seen, jnp.exp(masked - highest), 0.0)
+        raised = jnp.exp(masked - highest)
         own_raised = jnp.exp(own - highest)
-        denominator = jnp.sum(raised, axis=1, keepdims=True) + own_raised
-        weights = (raised / denominator).astype(jnp.bfloat16)
-        own_weight = (own_raised / denominator).astype(jnp.bfloat16).astype(jnp.float32)
+        inverse = 1.0 / (jnp.sum(raised, axis=1, keepdims=True) + own_raised)
+        weights = (raised * inverse).astype(jnp.bfloat16)
+        own_weight = (own_raised * inverse).astype(jnp.bfloat16).astype(jnp.float32)
         for r in range(rows_dev):
             part = slice(r * gq, (r + 1) * gq)
-            blended = jnp.dot(weights[part], vals[r], preferred_element_type=jnp.float32)
+            blended = jnp.dot(weights[part], vals[r, mine_keys], preferred_element_type=jnp.float32)
             orows[pl.ds(r, gq, stride=rows_dev), :] = blended + own_weight[part] * new_value[r:r + 1, :]
         att[j, gx] = orows[...].astype(jnp.bfloat16)
         for d in range(1, ZN):
@@ -208,11 +234,8 @@
 
     def step(t, _):
         for delay, stage in enumerate((project, across_x, attention, relay, output)):
-            if delay == 2:
-                @pl.when(t == 2)
-                def _():
-                    key_copy.wait()
-                    val_copy.wait()
+            if delay == 1:
+                pl.when(t == 1)(separate)
 
             @pl.when((t >= delay) & (t < groups + delay))
             def _(stage=stage, delay=delay):
@@ -256,21 +279,13 @@
     n = groups * pieces
     bf16, f32 = jnp.bfloat16, jnp.float32
 
-    half = hd // 2
-    frequency = 500000.0 ** (-(jnp.arange(half).astype(f32) * 2.0 / hd))
-    angles = lengths.astype(f32)[:, None] * frequency
-    cosine, sine = jnp.cos(angles), jnp.sin(angles)
-    cosine = jnp.concatenate([cosine, cosine], axis=1)
-    sine = jnp.concatenate([-sine, sine], axis=1)
-    limits = jnp.broadcast_to(jnp.repeat(lengths * groups, gq)[:, None], (rows_dev * gq, 128))
-
     anywhere = pl.BlockSpec(memory_space=pl.ANY)
     vmem = pl.BlockSpec(memory_space=pltpu.VMEM)
     dma = pltpu.SemaphoreType.DMA
     return pl.pallas_call(
         functools.partial(fused_kernel, (groups, gq, hd, piece, pieces, rows_dev)),
         out_shape=jax.ShapeDtypeStruct((half_rows, width), bf16),
-        in_specs=[anywhere] * 5 + [vmem] * 3,
+        in_specs=[anywhere] * 5 + [pl.BlockSpec(memory_space=pltpu.SMEM)],
         out_specs=vmem,
         scratch_shapes=[
             pltpu.VMEM((rows, depth), bf16),
@@ -285,8 +300,11 @@
             pltpu.VMEM((n, ZN - 1, rows_dev, piece), f32),
             pltpu.VMEM((rows_dev, block), f32),
             pltpu.VMEM((gq * rows_dev, hd), f32),
-            pltpu.VMEM((gq * rows_dev, context * groups), f32),
+            pltpu.VMEM((gq * rows_dev, context), f32),
             pltpu.VMEM((gq * rows_dev, hd), f32),
+            pltpu.VMEM((context * groups, hd), f32),
+            pltpu.VMEM((rows_dev, hd), f32),
+            pltpu.VMEM((rows_dev, hd), f32),
             pltpu.VMEM((groups, XN * ZN, gq * rows_dev, hd), bf16),
             pltpu.VMEM((rows, gq * hd), bf16),
             pltpu.VMEM((rows, width), f32),
@@ -307,7 +325,7 @@
         activations, qkv_weight, out_weight,
         key_cache.reshape(rows_dev, context * groups, hd),
         value_cache.reshape(rows_dev, context * groups, hd),
-        cosine, sine, limits,
+        lengths,
     )
 
 

time: 66.2 us -> 64 us (0.967)
  other arithmetic: 1.53 us -> 0 us
  local copies, waits for them, and re-layouts: 2.43 us -> 1.57 us
    broadcast_in_dim x3 -> x0, local copies, waits for them, and re-layouts: 0.87 us -> none  [the longest x2 0.79 us: fused(): jnp.broadcast_to(jnp.repeat(lengths * groups, gq)[:, None], (rows_dev * g...]
    mul x1 -> x0, other arithmetic: 0.74 us -> none  [fused(): lengths * groups]
    concatenate x1 -> x0, other arithmetic: 0.67 us -> none  [fused(): cosine = jnp.concatenate([cosine, cosine], axis=1)]
where the time goes in v2:
time: 64 us; the launch traced here: 63.9 us
  Pallas kernels  62.3 us (97%)
  local copies, waits for them, and re-layouts  1.57 us (2%)
    pallas_call x1, Pallas kernels, fused(): pl.pallas_call(functools.partial(fused_kernel, (groups, gq, hd, piece, pi...  62.3 us
    unnamed x1, local copies, waits for them, and re-layouts  1.57 us

profile of v2, /device:TPU:0, one launch (start us, length us, event | category | flops | bytes accessed | tf_op | source)
XLA Modules:
  0.0 63.9 jit_solution(11305778045929040760)
XLA Ops:
  0.0 62.3 %fused_attention.1 = bf16[32,2048]{1,0:T(8,128)(2,1)} custom-call(bf16[32,2048]{1,0:T(8,128)(2,1)} %act_hbm.1, bf16[2048,9216]{1,0:T(8,128)(2,1)} %wq_hbm.1, bf16[8192,2048]{1,0:T(8,128)(2,1)} %wo_hbm.1, bf16[8,1024,128]{2,1,0:T(8,128)(2,1)} %bitcast.2, bf16[8,1024,128]{2,1,0:T(8,128)(2,1)} %bitcast.3, s32[8]{0:T(128)} %len_ref.1), custom_call_target="tpu_custom_call" | custom-call | flops 4563402752 | bytes 71303168 | tf_op jit(solution)/shard_map/fused_attention/pallas_call | solution.py:285
  62.3 1.6 %copy.8 = bf16[32,2048]{1,0:T(8,128)(2,1)} copy(bf16[32,2048]{1,0:T(8,128)(2,1)} %fused_attention.1) | data formatting | bytes 262144

commit v3 on v2

--- a/solution.py
+++ b/solution.py
@@ -16,9 +16,9 @@
 
 def fused_kernel(
     dims, act_hbm, wq_hbm, wo_hbm, key_hbm, val_hbm, len_ref, out_ref,
-    act, wbuf, wo, keys, vals, xsend, xkeep, xrecv, zbuf, zrecv, proj, qrows, score, orows, split, cos_ref, sin_ref,
+    act, wbuf, wo, keys, vals, xsend, xkeep, xrecv, zbuf, znear, zsum, zfar, proj, qrows, score, orows, split, cos_ref, sin_ref,
     att, lhs, acc, psend, precv,
-    act_sem, w_sem, wo_sem, kv_sem, xs_sem, xr_sem, zs_sem, zr_sem,
+    act_sem, w_sem, wo_sem, kv_sem, xs_sem, xr_sem, ns_sem, nr_sem, fs_sem, fr_sem,
     azs_sem, azr_sem, axs_sem, axr_sem, ps_sem, pr_sem,
 ):
     groups, gq, hd, piece, pieces, rows_dev = dims
@@ -30,6 +30,8 @@
     z = lax.div(gx, XN)
     xpeer = z * XN + (1 - x)
     ypeer = 1 - gy
+    low = lax.rem(z, 2)
+    high = lax.div(z, 2)
 
     def zpeer(d):
         return lax.rem(z + d, ZN) * XN + x
@@ -56,10 +58,15 @@
             xsend.at[i], xrecv.at[i], xs_sem.at[i], xr_sem.at[i],
             device_id={"gx": xpeer}, device_id_type=MESH)
 
-    def z_copy(i, d):
-        return pltpu.make_async_remote_copy(
-            zbuf.at[i, lax.rem(z + d, ZN)], zrecv.at[i, d - 1], zs_sem.at[i, d - 1],
-            zr_sem.at[i, d - 1], device_id={"gx": zpeer(d)}, device_id_type=MESH)
+    def near_copy(i):
+        return pltpu.make_async_remote_copy(
+            zbuf.at[i, 1 - low], znear.at[i], ns_sem.at[i], nr_sem.at[i],
+            device_id={"gx": (2 * high + 1 - low) * XN + x}, device_id_type=MESH)
+
+    def far_copy(i):
+        return pltpu.make_async_remote_copy(
+            zsum.at[i, 1 - high], zfar.at[i], fs_sem.at[i], fr_sem.at[i],
+            device_id={"gx": (2 * (1 - high) + low) * XN + x}, device_id_type=MESH)
 
     def az_copy(j, d):
         return pltpu.make_async_remote_copy(
@@ -140,9 +147,18 @@
         def one(p, _):
             i = j * pieces + p
             x_copy(i).wait_recv()
-            zbuf[i] = xkeep[i] + xrecv[i]
-            for d in range(1, ZN):
-                z_copy(i, d).start()
+            for b in range(ZN):
+                zbuf[i, b % 2, b // 2] = xkeep[i, b] + xrecv[i, b]
+            near_copy(i).start()
+            return 0
+        lax.fori_loop(0, pieces, one, 0)
+
+    def across_z(j):
+        def one(p, _):
+            i = j * pieces + p
+            near_copy(i).wait_recv()
+            zsum[i] = zbuf[i, low] + znear[i]
+            far_copy(i).start()
             return 0
         lax.fori_loop(0, pieces, one, 0)
 
@@ -163,9 +179,8 @@
     def attention(j):
         for p in range(pieces):
             i = j * pieces + p
-            for d in range(1, ZN):
-                z_copy(i, d).wait_recv()
-            total = zbuf[i, z] + zrecv[i, 0] + zrecv[i, 1] + zrecv[i, 2]
+            far_copy(i).wait_recv()
+            total = zsum[i, high] + zfar[i]
             proj[:, p * piece:(p + 1) * piece] = total.astype(jnp.bfloat16).astype(jnp.float32)
 
         def turned(h):
@@ -233,7 +248,8 @@
         lax.fori_loop(0, acc.shape[1] // TILE, one, 0)
 
     def step(t, _):
-        for delay, stage in enumerate((project, across_x, attention, relay, output)):
+        for delay, stage in enumerate(
+                (project, across_x, across_z, attention, relay, output)):
             if delay == 1:
                 pl.when(t == 1)(separate)
 
@@ -241,7 +257,7 @@
             def _(stage=stage, delay=delay):
                 stage(t - delay)
         return 0
-    lax.fori_loop(0, groups + 4, step, 0)
+    lax.fori_loop(0, groups + 5, step, 0)
 
     psend[...] = acc[theirs, :].astype(jnp.bfloat16)
     last = pltpu.make_async_remote_copy(
@@ -255,8 +271,8 @@
         for p in range(pieces):
             i = j * pieces + p
             x_copy(i).wait_send()
-            for d in range(1, ZN):
-                z_copy(i, d).wait_send()
+            near_copy(i).wait_send()
+            far_copy(i).wait_send()
         for d in range(1, ZN):
             az_copy(j, d).wait_send()
         for d in range(ZN):
@@ -296,8 +312,10 @@
             pltpu.VMEM((n, ZN, rows_dev, piece), f32),
             pltpu.VMEM((n, ZN, rows_dev, piece), f32),
             pltpu.VMEM((n, ZN, rows_dev, piece), f32),
-            pltpu.VMEM((n, ZN, rows_dev, piece), f32),
-            pltpu.VMEM((n, ZN - 1, rows_dev, piece), f32),
+            pltpu.VMEM((n, 2, ZN // 2, rows_dev, piece), f32),
+            pltpu.VMEM((n, ZN // 2, rows_dev, piece), f32),
+            pltpu.VMEM((n, ZN // 2, rows_dev, piece), f32),
+            pltpu.VMEM((n, rows_dev, piece), f32),
             pltpu.VMEM((rows_dev, block), f32),
             pltpu.VMEM((gq * rows_dev, hd), f32),
             pltpu.VMEM((gq * rows_dev, context), f32),
@@ -311,7 +329,7 @@
             pltpu.VMEM((half_rows, width), bf16),
             pltpu.VMEM((half_rows, width), bf16),
             dma((3,)), dma((SLOTS,)), dma((groups,)), dma((2,)),
-            dma((n,)), dma((n,)), dma((n, ZN - 1)), dma((n, ZN - 1)),
+            dma((n,)), dma((n,)), dma((n,)), dma((n,)), dma((n,)), dma((n,)),
             dma((groups, ZN - 1)), dma((groups, ZN - 1)), dma((groups, ZN)), dma((groups, ZN)),
             dma, dma,
         ],

time: 64 us -> 64.9 us (1.014)
  Pallas kernels: 62.3 us -> 63.2 us
    pallas_call x1, Pallas kernels: 62.3 us -> 63.2 us  [fused(): pl.pallas_call(functools.partial(fused_kernel, (groups, gq, hd, piece, pi...]
where the time goes in v3:
time: 64.9 us; the launch traced here: 64.7 us
  Pallas kernels  63.2 us (97%)
  local copies, waits for them, and re-layouts  1.57 us (2%)
    pallas_call x1, Pallas kernels, fused(): pl.pallas_call(functools.partial(fused_kernel, (groups, gq, hd, piece, pi...  63.2 us
    unnamed x1, local copies, waits for them, and re-layouts  1.57 us

profile of v3, /device:TPU:0, one launch (start us, length us, event | category | flops | bytes accessed | tf_op | source)
XLA Modules:
  0.0 64.7 jit_solution(1004222693710862055)
XLA Ops:
  0.0 63.2 %fused_attention.1 = bf16[32,2048]{1,0:T(8,128)(2,1)} custom-call(bf16[32,2048]{1,0:T(8,128)(2,1)} %act_hbm.1, bf16[2048,9216]{1,0:T(8,128)(2,1)} %wq_hbm.1, bf16[8192,2048]{1,0:T(8,128)(2,1)} %wo_hbm.1, bf16[8,1024,128]{2,1,0:T(8,128)(2,1)} %bitcast.2, bf16[8,1024,128]{2,1,0:T(8,128)(2,1)} %bitcast.3, s32[8]{0:T(128)} %len_ref.1), custom_call_target="tpu_custom_call" | custom-call | flops 4563402752 | bytes 71303168 | tf_op jit(solution)/shard_map/fused_attention/pallas_call | solution.py:301
  63.2 1.6 %copy.8 = bf16[32,2048]{1,0:T(8,128)(2,1)} copy(bf16[32,2048]{1,0:T(8,128)(2,1)} %fused_attention.1) | data formatting | bytes 262144

commit v4 on v2

--- a/solution.py
+++ b/solution.py
@@ -134,7 +134,6 @@
                 w_copy(i + SLOTS).start()
             return 0
         lax.fori_loop(0, pieces, one, 0)
-        wo_copy(j).start()
 
     def across_x(j):
         def one(p, _):
@@ -161,6 +160,7 @@
         lax.fori_loop(0, rows_dev, one, 0)
 
     def attention(j):
+        wo_copy(j).start()
         for p in range(pieces):
             i = j * pieces + p
             for d in range(1, ZN):
@@ -233,15 +233,16 @@
         lax.fori_loop(0, acc.shape[1] // TILE, one, 0)
 
     def step(t, _):
-        for delay, stage in enumerate((project, across_x, attention, relay, output)):
-            if delay == 1:
+        for delay, stage in (
+                (0, project), (2, across_x), (3, attention), (4, relay), (5, output)):
+            if delay == 2:
                 pl.when(t == 1)(separate)
 
             @pl.when((t >= delay) & (t < groups + delay))
             def _(stage=stage, delay=delay):
                 stage(t - delay)
         return 0
-    lax.fori_loop(0, groups + 4, step, 0)
+    lax.fori_loop(0, groups + 5, step, 0)
 
     psend[...] = acc[theirs, :].astype(jnp.bfloat16)
     last = pltpu.make_async_remote_copy(

time: 64 us -> 66.5 us (1.039)
  Pallas kernels: 62.3 us -> 64.8 us
    pallas_call x1, Pallas kernels: 62.3 us -> 64.8 us  [fused(): pl.pallas_call(functools.partial(fused_kernel, (groups, gq, hd, piece, pi...]
where the time goes in v4:
time: 66.5 us; the launch traced here: 66.3 us
  Pallas kernels  64.8 us (97%)
  local copies, waits for them, and re-layouts  1.57 us (2%)
    pallas_call x1, Pallas kernels, fused(): pl.pallas_call(functools.partial(fused_kernel, (groups, gq, hd, piece, pi...  64.8 us
    unnamed x1, local copies, waits for them, and re-layouts  1.57 us

profile of v4, /device:TPU:0, one launch (start us, length us, event | category | flops | bytes accessed | tf_op | source)
XLA Modules:
  0.0 66.3 jit_solution(15637652616277627007)
XLA Ops:
  0.0 64.8 %fused_attention.1 = bf16[32,2048]{1,0:T(8,128)(2,1)} custom-call(bf16[32,2048]{1,0:T(8,128)(2,1)} %act_hbm.1, bf16[2048,9216]{1,0:T(8,128)(2,1)} %wq_hbm.1, bf16[8192,2048]{1,0:T(8,128)(2,1)} %wo_hbm.1, bf16[8,1024,128]{2,1,0:T(8,128)(2,1)} %bitcast.2, bf16[8,1024,128]{2,1,0:T(8,128)(2,1)} %bitcast.3, s32[8]{0:T(128)} %len_ref.1), custom_call_target="tpu_custom_call" | custom-call | flops 4563402752 | bytes 71303168 | tf_op jit(solution)/shard_map/fused_attention/pallas_call | solution.py:286
  64.8 1.6 %copy.8 = bf16[32,2048]{1,0:T(8,128)(2,1)} copy(bf16[32,2048]{1,0:T(8,128)(2,1)} %fused_attention.1) | data formatting | bytes 262144
